TPU v7x, 128 devices: a whole 4x4x4 slice. The times are simulated.
128 devices in a mesh: row: 8 (over z, core), col: 16 (over y, x).
Axes of the slice: x: 4, y: 4, z: 4, core: 2. Of those that a mesh axis runs over, the one named last changes fastest.
Arguments:
- operator: float32 [16384, 16384], P('row', 'col'), may hold values from -0.046875 to 0.046875
- vectors: float32 [16384, 256], P('row', 'col'), may hold values from -6 to 6
- owner_map: int32 [11264, 1], P(('row', 'col')), may hold values from 0 to 15; in each aligned block of 88 rows (0 to 87, 88 to 175, ...) at most 16 rows name the same one
- coupling: float32 [8, 512, 1024], P('row', 'col'), may hold values from -0.1875 to 0.1875
- ancestors: int32 [8, 16, 512], P('row', 'col'), may hold values from 0 to 1535, as said below
- leaf_modes: float32 [8, 16, 2048, 256], P('row', 'col'), may hold values from -0.375 to 0.375
- constraint_modes: float32 [8, 16, 2048, 512], P('row', 'col'), may hold values from -0.25 to 0.25
Outputs:
- separators: float32 [8, 512, 256], P('row', 'col')
- interiors: float32 [8, 16, 2048, 256], P('row', 'col')
Inputs may be any that keep to these rules, and one draw needn't show every extreme that they name: `owner_map`: in each aligned block of 88 rows no leaf is named more than 16 times, a bound that some block reaches. `ancestors`: the 512 indices of one leaf are distinct.
All inputs are finite; a program needn't handle non-finite values.
Results may differ from a plain program's by a relative error of at most 0.00007.
Values sent between devices are 32-bit elements; how exact they have to be, the bound alone decides.
A program may use at most 64 MiB of HBM per device.

v0:
```python
import jax
import jax.numpy as jnp
from jax import lax
from jax.sharding import PartitionSpec as P

highest = lax.Precision.HIGHEST


def slot_ranks(owned_rows, fanout):
    onehot = (owned_rows[..., None] == jnp.arange(fanout, dtype=jnp.int32)).astype(jnp.int32)
    running = jnp.cumsum(onehot, axis=-2)
    return jnp.sum(running * onehot, axis=-1) - 1


def on_device(operator, vectors, owner_map, coupling, ancestors, leaf_modes, constraint_modes):
    fanout = lax.axis_size("col")
    mode_local = owner_map.shape[0]
    separator_local = coupling.shape[1]
    mode_count = leaf_modes.shape[3]
    slot_count = mode_count // fanout
    mode_matrix = leaf_modes[0, 0]
    partial_adjoint = lax.dot_general(
        operator,
        lax.all_gather(vectors, "col", axis=1, tiled=True),
        (((0,), (0,)), ((), ())),
        precision=highest,
        preferred_element_type=jnp.float32,
    )
    adjoint = lax.psum(partial_adjoint, "row")
    forward = jnp.dot(operator, adjoint, precision=highest, preferred_element_type=jnp.float32)
    vector_count = forward.shape[1]
    local_rows = lax.psum_scatter(forward, "col", scatter_dimension=0, tiled=True)
    mode_rows = local_rows[:mode_local]
    separator_raw = local_rows[mode_local : mode_local + separator_local]
    top_local = local_rows[mode_local + separator_local :]
    owned_here = owner_map[:, 0]
    target = owned_here * slot_count + slot_ranks(owned_here, fanout)
    source = (
        jnp.full((fanout * slot_count,), mode_local, jnp.int32)
        .at[target]
        .set(jnp.arange(mode_local, dtype=jnp.int32))
    )
    outgoing = jnp.take(mode_rows, source, axis=0, mode="fill", fill_value=0.0).reshape(
        fanout, slot_count, vector_count
    )
    received = lax.all_to_all(outgoing, "col", split_axis=0, concat_axis=0, tiled=True)
    flattened = received.reshape(mode_count, received.shape[2])
    modal_sum = jnp.dot(
        mode_matrix, flattened, precision=highest, preferred_element_type=jnp.float32
    )
    top_gathered = lax.all_gather(top_local, ("row", "col"), axis=0, tiled=True)
    separators = separator_raw + jnp.dot(
        coupling[0], top_gathered, precision=highest, preferred_element_type=jnp.float32
    )
    separator_all = lax.all_gather(separators, "col", axis=0, tiled=True)
    candidates = jnp.concatenate([top_gathered, separator_all], axis=0)
    picked = jnp.take(candidates, ancestors[0, 0], axis=0)
    interiors = modal_sum + jnp.dot(
        constraint_modes[0, 0], picked, precision=highest, preferred_element_type=jnp.float32
    )
    return (separators[None], interiors[None, None])


def solution(mesh):
    in_specs = (
        P("row", "col"),
        P("row", "col"),
        P(("row", "col"), None),
        P("row", "col", None),
        P("row", "col", None),
        P("row", "col", None, None),
        P("row", "col", None, None),
    )
    out_specs = (P("row", "col", None), P("row", "col", None, None))
    return jax.shard_map(
        on_device, mesh=mesh, in_specs=in_specs, out_specs=out_specs, check_vma=False
    )
```

profile of v0, /device:TPU:0, one launch (start us, length us, event | category | flops | bytes accessed | tf_op | source)
XLA Modules:
  0.0 350.4 jit_solution(7148521597005728503)
XLA Ops:
  7.2 0.0 all-gather.3.cloned.1.call-start
  7.2 0.7 all-gather.3.cloned.1.call-update
  7.9 0.0 all-reduce.2.cloned.1.call-start
  8.0 49.5 %all-gather.3.cloned.1.call-done = f32[2048,256]{0,1:T(8,128)} async-done(((f32[2048,16]{0,1:T(8,128)}), f32[2048,256]{0,1:T(8,128)}) %all-gather.3.cloned.1.call-update) | async-done | bytes 2097168 | tf_op jit(solution)/shard_map/all_gather | solution.py:24
  57.4 17.0 %fusion.14 = f32[1024,256]{1,0:T(8,128)} fusion(f32[2048,1024]{1,0:T(8,128)} %param.7, f32[2048,256]{0,1:T(8,128)} %all-gather.3.cloned.1.call-done), kind=kOutput, calls=%fused_computation.33 | convolution fusion | flops 6442450944 | bytes 11534336 | tf_op jit(solution)/shard_map/dot_general | solution.py:22
  74.4 0.0 all-reduce.2.cloned.1.call-update
  74.5 0.2 reduce-scatter.2.cloned.1.call-start
  74.7 62.0 %all-reduce.2.cloned.1.call-done = f32[1024,256]{1,0:T(8,128)} async-done(((f32[1024,256]{1,0:T(8,128)}), f32[1024,256]{1,0:T(8,128)}) %all-reduce.2.cloned.1.call-update) | async-done | bytes 1048592 | tf_op jit(solution)/shard_map/psum | solution.py:29
  136.7 17.1 %convolution_bitcast_fusion = f32[2048,256]{0,1:T(8,128)} fusion(f32[1024,256]{1,0:T(8,128)} %all-reduce.2.cloned.1.call-done, f32[2048,1024]{1,0:T(8,128)} %param.7), kind=kOutput, calls=%fused_computation.7 | convolution fusion | flops 6442450944 | bytes 11534336 | tf_op jit(solution)/shard_map/dot_general | solution.py:30
  153.8 0.0 all-gather.5.cloned.1.call-start
  153.8 73.4 %reduce-scatter.2.cloned.1.call-done = f32[128,256]{0,1:T(8,128)} async-done(((f32[2048,256]{0,1:T(8,128)}), f32[128,256]{0,1:T(8,128)}) %reduce-scatter.2.cloned.1.call-update) | async-done | bytes 131088 | tf_op jit(solution)/shard_map/reduce_scatter | solution.py:32
  227.3 1.1 slice.17
  228.3 0.7 copy.19
  229.0 0.1 fusion.9
  229.1 0.1 reduce_window_sum.11
  229.2 0.2 select_reduce_fusion
  229.4 0.8 scatter_custom_fusion
  230.3 0.1 broadcast_in_dim.37
  230.5 1.0 copy.21
  231.5 1.0 gather_fusion
  232.4 0.8 broadcast_select_fusion
  233.2 4.9 %all-to-all-start = ((f32[16,16,256]{2,1,0:T(8,128)}), f32[16,16,256]{2,1,0:T(8,128)}, u32[]{:S(2)}, u32[]{:S(2)}) async-start(f32[16,16,256]{2,1,0:T(8,128)} %broadcast_select_fusion), calls=%async_computation.1 | async-start | bytes 524288 | tf_op jit(solution)/shard_map/all_to_all | solution.py:46
  238.1 55.6 %all-gather.5.cloned.1.call-done = f32[1024,256]{1,0:T(8,128)} async-done(((f32[8,256]{1,0:T(8,128)}), f32[1024,256]{1,0:T(8,128)}) %all-gather.5.cloned.1.call-update) | async-done | bytes 1048592 | tf_op jit(solution)/shard_map/all_gather | solution.py:51
  293.7 3.1 fusion.4
  296.9 0.1 copy.22
  296.9 0.7 copy.23
  297.6 22.3 %all_gather.11 = f32[512,256]{1,0:T(8,128)S(1)} all-gather(f32[32,256]{1,0:T(8,128)S(1)} %copy.22), channel_id=1, replica_groups=mesh['row'=8,'col'=16] {'col'}, dimensions={0}, use_global_device_ids=true | all-gather | bytes 557056 | tf_op jit(solution)/shard_map/all_gather | solution.py:55
  319.9 1.2 pad_maximum_fusion
  321.1 3.0 gather_fusion.1
  324.1 10.4 %fusion = f32[256,2048]{1,0:T(8,128)} fusion(f32[1,1,2048,512]{3,2,1,0:T(8,128)} %param.13, f32[512,256]{1,0:T(8,128)S(1)} %gather_fusion.1, pred[512]{0:T(512)(128)(4,1)S(1)} %compare_and_fusion), kind=kOutput, calls=%fused_computation.3 | convolution fusion | flops 3221356544 | bytes 6816256 | tf_op jit(solution)/shard_map/dot_general | solution.py:58
  334.5 6.5 %fusion.2 = f32[1,1,2048,256]{2,3,1,0:T(8,128)} fusion(f32[256,2048]{1,0:T(8,128)} %fusion, f32[256,256]{1,0:T(8,128)} %bitcast.8, f32[1,1,2048,256]{3,2,1,0:T(8,128)S(1)} %copy-done), kind=kOutput, calls=%fused_computation.6 | convolution fusion | flops 1611137024 | bytes 6553600 | tf_op jit(solution)/shard_map/dot_general | solution.py:48
  341.0 2.9 copy.24
  (23 shorter events, 0.1 us)
Async XLA Ops:
  7.2 327.3 %copy-start = (f32[1,1,2048,256]{3,2,1,0:T(8,128)S(1)}, f32[1,1,2048,256]{3,2,1,0:T(8,128)}, u32[]{:S(2)}) copy-start(f32[1,1,2048,256]{3,2,1,0:T(8,128)} %param.12) | copy-start | bytes 6291460
  7.2 50.3 %all-gather.3.cloned.1.call-start = ((), (), s32[]{:S(2)}) async-start(), calls=%async_computation.2 | async-start | bytes 2228224 | tf_op jit(solution)/shard_map/all_gather | solution.py:24
  7.9 128.8 %all-reduce.2.cloned.1.call-start = ((), (), s32[]{:S(2)}) async-start(), calls=%async_computation.3 | async-start | bytes 2097152 | tf_op jit(solution)/shard_map/psum | solution.py:29
  74.5 152.8 %reduce-scatter.2.cloned.1.call-start = ((), (), s32[]{:S(2)}) async-start(), calls=%async_computation.4 | async-start | bytes 2228224 | tf_op jit(solution)/shard_map/reduce_scatter | solution.py:32
  153.7 75.3 %copy-start.5 = (s32[88,1]{0,1:T(1,128)S(1)}, s32[88,1]{0,1:T(1,128)}, u32[]{:S(2)}) copy-start(s32[88,1]{0,1:T(1,128)} %param.9) | copy-start | bytes 1060
  153.8 76.7 %copy-start.4 = (s32[1,1,512]{2,1,0:T(1,128)S(1)}, s32[1,1,512]{2,1,0:T(1,128)}, u32[]{:S(2)}) copy-start(s32[1,1,512]{2,1,0:T(1,128)} %param.11) | copy-start | bytes 6148
  153.8 140.0 %copy-start.3 = (f32[1,32,1024]{2,1,0:T(8,128)S(1)}, f32[1,32,1024]{2,1,0:T(8,128)}, u32[]{:S(2)}) copy-start(f32[1,32,1024]{2,1,0:T(8,128)} %param.10) | copy-start | bytes 393220
  153.8 140.0 %all-gather.5.cloned.1.call-start = ((), (), s32[]{:S(2)}) async-start(), calls=%async_computation.5 | async-start | bytes 1056768 | tf_op jit(solution)/shard_map/all_gather | solution.py:51
  227.2 66.5 %copy-start.2 = (f32[128,256]{0,1:T(8,128)S(1)}, f32[128,256]{0,1:T(8,128)}, u32[]{:S(2)}) copy-start(f32[128,256]{0,1:T(8,128)} %reduce-scatter.2.cloned.1.call-done) | copy-start | bytes 393220
  233.2 101.3 %all-to-all-start = ((f32[16,16,256]{2,1,0:T(8,128)}), f32[16,16,256]{2,1,0:T(8,128)}, u32[]{:S(2)}, u32[]{:S(2)}) async-start(f32[16,16,256]{2,1,0:T(8,128)} %broadcast_select_fusion), calls=%async_computation.1 | async-start | bytes 524288 | tf_op jit(solution)/shard_map/all_to_all | solution.py:46
  293.7 26.1 %copy-start.1 = (f32[1024,256]{1,0:T(8,128)S(1)}, f32[1024,256]{1,0:T(8,128)}, u32[]{:S(2)}) copy-start(f32[1024,256]{1,0:T(8,128)} %all-gather.5.cloned.1.call-done) | copy-start | bytes 3145732
Sparse Core Ops, SparseCore 0:
  10.2 47.2 all-gather.2
  74.6 62.0 all-reduce.1
  153.9 73.3 reduce-scatter.1
  230.8 62.8 all-gather.4
where the time goes:
time: 351 us; the launch traced here: 350 us
  waiting for transfers between devices  241 us (69%)
  matrix products  54.1 us (15%)
  blocking collectives  22.3 us (6%)
  between operations  13.9 us (4%)
  local copies, waits for them, and re-layouts  11.3 us (3%)
  starting transfers between devices  5.23 us (1%)
    reduce_scatter x1, waiting for transfers between devices, on_device(): lax.psum_scatter(forward, 'col', scatter_dimension=0, tiled=True)  73.4 us
    psum x1, waiting for transfers between devices, on_device(): adjoint = lax.psum(partial_adjoint, 'row')  62 us
    all_gather x1, waiting for transfers between devices, on_device(): top_gathered = lax.all_gather(top_local, ('row', 'col'), axis=0, tiled=True)  55.6 us
    all_gather x1, waiting for transfers between devices, on_device(): lax.all_gather(vectors, 'col', axis=1, tiled=True)  49.5 us
    all_gather x1, blocking collectives, on_device(): separator_all = lax.all_gather(separators, 'col', axis=0, tiled=True)  22.3 us
    dot_general x1, matrix products, on_device(): jnp.dot(operator, adjoint, precision=highest, preferred_element_type=jnp....  17.1 us
    dot_general x1, matrix products, on_device(): lax.dot_general(operator, lax.all_gather(vectors, 'col', axis=1, tiled=Tr...  17 us
    dot_general x1, matrix products, on_device(): jnp.dot(constraint_modes[0, 0], picked, precision=highest, preferred_elem...  10.4 us
  transfers between devices with their start and end apart: 5, of which 4 were waited for; matrix products, arithmetic and copies ran while one was open for 6% of the time, Pallas kernels for 0%

commit v1 on v0

--- a/solution.py
+++ b/solution.py
@@ -4,6 +4,27 @@
 from jax.sharding import PartitionSpec as P
 
 highest = lax.Precision.HIGHEST
+
+
+def collect(x, axis, dim):
+    size, index, extent = (lax.axis_size(axis), lax.axis_index(axis), x.shape[dim])
+    upward = [(i, (i + 1) % size) for i in range(size)]
+    left = [(i, (i - 1) % size) for i in range(size)]
+    whole = jnp.zeros((*x.shape[:dim], size * extent, *x.shape[dim + 1 :]), x.dtype)
+    whole = lax.dynamic_update_slice_in_dim(whole, x, index * extent, axis=dim)
+    from_left = from_right = x
+    middle = size // 2
+    for lap in range(1, middle + 1):
+        from_left = lax.ppermute(from_left, axis, upward)
+        whole = lax.dynamic_update_slice_in_dim(
+            whole, from_left, (index - lap) % size * extent, axis=dim
+        )
+        if lap < size - middle:
+            from_right = lax.ppermute(from_right, axis, left)
+            whole = lax.dynamic_update_slice_in_dim(
+                whole, from_right, (index + lap) % size * extent, axis=dim
+            )
+    return whole
 
 
 def slot_ranks(owned_rows, fanout):
@@ -21,7 +42,7 @@
     mode_matrix = leaf_modes[0, 0]
     partial_adjoint = lax.dot_general(
         operator,
-        lax.all_gather(vectors, "col", axis=1, tiled=True),
+        collect(vectors, "col", 1),
         (((0,), (0,)), ((), ())),
         precision=highest,
         preferred_element_type=jnp.float32,

time: 351 us -> 355 us (1.011)
  starting transfers between devices: 5.23 us -> 43 us
  waiting for transfers between devices: 241 us -> 219 us
  matrix products: 54.1 us -> 41.3 us
    all_gather x1 -> x0, waiting for transfers between devices: 49.5 us -> none  [on_device(): lax.all_gather(vectors, 'col', axis=1, tiled=True)]
    ppermute x0 -> x15, starting transfers between devices: none -> 37.8 us  [the longest x7 36.2 us: collect(): from_right = lax.ppermute(from_right, axis, left)]
    ppermute x0 -> x15, waiting for transfers between devices: none -> 30.3 us  [the longest x8 30.3 us: collect(): from_left = lax.ppermute(from_left, axis, upward)]
    dot_general x1, matrix products: 17 us -> 10.4 us  [on_device(): lax.dot_general(operator, collect(vectors, 'col', 1), (((0,), (0,)), ((),...]
    dot_general x1, matrix products: 17.1 us -> 10.9 us  [on_device(): jnp.dot(operator, adjoint, precision=highest, preferred_element_type=jnp....]
  transfers between devices with their start and end apart: 5 -> 19, of which waited for: 4 -> 11; matrix products, arithmetic and copies ran while one was open for 6% -> 6% of each run, Pallas kernels for 0% -> 0%
where the time goes in v1:
time: 355 us; the launch traced here: 354 us
  waiting for transfers between devices  219 us (62%)
  starting transfers between devices  43 us (12%)
  matrix products  41.3 us (12%)
  blocking collectives  22.3 us (6%)
  between operations  14 us (4%)
  local copies, waits for them, and re-layouts  11.7 us (3%)
    reduce_scatter x1, waiting for transfers between devices, on_device(): lax.psum_scatter(forward, 'col', scatter_dimension=0, tiled=True)  73.4 us
    psum x1, waiting for transfers between devices, on_device(): adjoint = lax.psum(partial_adjoint, 'row')  59.8 us
    all_gather x1, waiting for transfers between devices, on_device(): top_gathered = lax.all_gather(top_local, ('row', 'col'), axis=0, tiled=True)  55.7 us
    ppermute x7, starting transfers between devices, collect(): from_right = lax.ppermute(from_right, axis, left)  36.2 us
    ppermute x8, waiting for transfers between devices, collect(): from_left = lax.ppermute(from_left, axis, upward)  30.3 us
    all_gather x1, blocking collectives, on_device(): separator_all = lax.all_gather(separators, 'col', axis=0, tiled=True)  22.3 us
    dot_general x1, matrix products, on_device(): jnp.dot(operator, adjoint, precision=highest, preferred_element_type=jnp....  10.9 us
    dot_general x1, matrix products, on_device(): lax.dot_general(operator, collect(vectors, 'col', 1), (((0,), (0,)), ((),...  10.4 us
  transfers between devices with their start and end apart: 19, of which 11 were waited for; matrix products, arithmetic and copies ran while one was open for 6% of the time, Pallas kernels for 0%

profile of v1, /device:TPU:0, one launch (start us, length us, event | category | flops | bytes accessed | tf_op | source)
XLA Modules:
  0.0 354.2 jit_solution(12077835336352278363)
XLA Ops:
  7.2 1.6 collective-permute-start
  8.9 3.8 %collective-permute-start.1 = (f32[2048,16]{0,1:T(8,128)}, f32[2048,16]{0,1:T(8,128)S(1)}, u32[]{:S(2)}, u32[]{:S(2)}) collective-permute-start(f32[2048,16]{0,1:T(8,128)} %param.8), channel_id=1, source_target_pairs={{0,15},{1,0},{2,1},{3,2},{4,3},{5,4},{6,5},{7,6},{8,7},{9,8},{10,9... | collective-permute-start | bytes 393224 | tf_op jit(solution)/shard_map/ppermute | solution.py:23
  12.9 3.4 collective-permute-done
  16.3 5.3 %collective-permute-start.3 = (f32[2048,16]{0,1:T(8,128)S(1)}, f32[2048,16]{0,1:T(8,128)S(1)}, u32[]{:S(2)}, u32[]{:S(2)}) collective-permute-start(f32[2048,16]{0,1:T(8,128)S(1)} %collective-permute-done.1), channel_id=1, source_target_pairs={{0,15},{1,0},{2,1},{3,2},{4,3},{5,4},{6,5},{7,6},{8,7},{9,8},{10,9... | collective-permute-start | bytes 393224 | tf_op jit(solution)/shard_map/ppermute | solution.py:23
  21.7 2.9 collective-permute-done.2
  24.6 5.3 %collective-permute-start.5 = (f32[2048,16]{0,1:T(8,128)S(1)}, f32[2048,16]{0,1:T(8,128)S(1)}, u32[]{:S(2)}, u32[]{:S(2)}) collective-permute-start(f32[2048,16]{0,1:T(8,128)S(1)} %collective-permute-done.3), channel_id=1, source_target_pairs={{0,15},{1,0},{2,1},{3,2},{4,3},{5,4},{6,5},{7,6},{8,7},{9,8},{10,9... | collective-permute-start | bytes 393224 | tf_op jit(solution)/shard_map/ppermute | solution.py:23
  30.0 2.9 collective-permute-done.4
  32.9 5.3 %collective-permute-start.7 = (f32[2048,16]{0,1:T(8,128)S(1)}, f32[2048,16]{0,1:T(8,128)S(1)}, u32[]{:S(2)}, u32[]{:S(2)}) collective-permute-start(f32[2048,16]{0,1:T(8,128)S(1)} %collective-permute-done.5), channel_id=1, source_target_pairs={{0,15},{1,0},{2,1},{3,2},{4,3},{5,4},{6,5},{7,6},{8,7},{9,8},{10,9... | collective-permute-start | bytes 393224 | tf_op jit(solution)/shard_map/ppermute | solution.py:23
  38.3 2.9 collective-permute-done.6
  41.2 5.3 %collective-permute-start.9 = (f32[2048,16]{0,1:T(8,128)S(1)}, f32[2048,16]{0,1:T(8,128)S(1)}, u32[]{:S(2)}, u32[]{:S(2)}) collective-permute-start(f32[2048,16]{0,1:T(8,128)S(1)} %collective-permute-done.7), channel_id=1, source_target_pairs={{0,15},{1,0},{2,1},{3,2},{4,3},{5,4},{6,5},{7,6},{8,7},{9,8},{10,9... | collective-permute-start | bytes 393224 | tf_op jit(solution)/shard_map/ppermute | solution.py:23
  46.6 2.9 collective-permute-done.8
  49.5 5.3 %collective-permute-start.11 = (f32[2048,16]{0,1:T(8,128)S(1)}, f32[2048,16]{0,1:T(8,128)S(1)}, u32[]{:S(2)}, u32[]{:S(2)}) collective-permute-start(f32[2048,16]{0,1:T(8,128)S(1)} %collective-permute-done.9), channel_id=1, source_target_pairs={{0,15},{1,0},{2,1},{3,2},{4,3},{5,4},{6,5},{7,6},{8,7},{9,8},{10,9... | collective-permute-start | bytes 393224 | tf_op jit(solution)/shard_map/ppermute | solution.py:23
  54.8 3.5 collective-permute-done.10
  58.4 5.7 %collective-permute-start.13 = (f32[2048,16]{0,1:T(8,128)S(1)}, f32[2048,16]{0,1:T(8,128)S(1)}, u32[]{:S(2)}, u32[]{:S(2)}) collective-permute-start(f32[2048,16]{0,1:T(8,128)S(1)} %collective-permute-done.11), channel_id=1, source_target_pairs={{0,15},{1,0},{2,1},{3,2},{4,3},{5,4},{6,5},{7,6},{8,7},{9,8},{10,9... | collective-permute-start | bytes 393224 | tf_op jit(solution)/shard_map/ppermute | solution.py:23
  64.1 3.6 %collective-permute-done.12 = f32[2048,16]{0,1:T(8,128)S(1)} collective-permute-done((f32[2048,16]{0,1:T(8,128)S(1)}, f32[2048,16]{0,1:T(8,128)S(1)}, u32[]{:S(2)}, u32[]{:S(2)}) %collective-permute-start.12) | collective-permute-done | bytes 131104 | tf_op jit(solution)/shard_map/ppermute | solution.py:18
  67.7 8.2 %collective-permute-done.14 = f32[2048,16]{0,1:T(8,128)S(1)} collective-permute-done((f32[2048,16]{0,1:T(8,128)S(1)}, f32[2048,16]{0,1:T(8,128)S(1)}, u32[]{:S(2)}, u32[]{:S(2)}) %collective-permute-start.14) | collective-permute-done | bytes 131104 | tf_op jit(solution)/shard_map/ppermute | solution.py:18
  76.0 10.4 %convolution_bitcast_fusion.1 = f32[1024,256]{0,1:T(8,128)} fusion(f32[2048,256]{0,1:T(8,128)S(1)} %constant_dynamic-update-slice_fusion, f32[2048,1024]{1,0:T(8,128)} %param.7), kind=kOutput, calls=%fused_computation.10 | convolution fusion | flops 6442450944 | bytes 11534336 | tf_op jit(solution)/shard_map/dot_general | solution.py:43
  86.6 59.8 %all-reduce.2.cloned.1.call-done = f32[1024,256]{0,1:T(8,128)} async-done(((f32[1024,256]{0,1:T(8,128)}), f32[1024,256]{0,1:T(8,128)}) %all-reduce.2.cloned.1.call-update) | async-done | bytes 1048592 | tf_op jit(solution)/shard_map/psum | solution.py:50
  146.5 10.9 %convolution_bitcast_fusion = f32[2048,256]{0,1:T(8,128)} fusion(f32[1024,256]{0,1:T(8,128)} %all-reduce.2.cloned.1.call-done, f32[2048,1024]{1,0:T(8,128)} %param.7), kind=kOutput, calls=%fused_computation.7 | convolution fusion | flops 6442450944 | bytes 11534336 | tf_op jit(solution)/shard_map/dot_general | solution.py:51
  157.4 73.4 %reduce-scatter.2.cloned.1.call-done = f32[128,256]{0,1:T(8,128)} async-done(((f32[2048,256]{0,1:T(8,128)}), f32[128,256]{0,1:T(8,128)}) %reduce-scatter.2.cloned.1.call-update) | async-done | bytes 131088 | tf_op jit(solution)/shard_map/reduce_scatter | solution.py:53
  230.9 1.1 slice.17
  234.1 1.0 copy.21
  235.1 1.0 gather_fusion
  236.9 4.9 %all-to-all-start = ((f32[16,16,256]{2,1,0:T(8,128)}), f32[16,16,256]{2,1,0:T(8,128)}, u32[]{:S(2)}, u32[]{:S(2)}) async-start(f32[16,16,256]{2,1,0:T(8,128)} %broadcast_select_fusion), calls=%async_computation.1 | async-start | bytes 524288 | tf_op jit(solution)/shard_map/all_to_all | solution.py:67
  241.8 55.7 %all-gather.2.cloned.1.call-done = f32[1024,256]{1,0:T(8,128)} async-done(((f32[8,256]{1,0:T(8,128)}), f32[1024,256]{1,0:T(8,128)}) %all-gather.2.cloned.1.call-update) | async-done | bytes 1048592 | tf_op jit(solution)/shard_map/all_gather | solution.py:72
  297.5 3.1 fusion.4
  300.7 22.3 %all_gather.7 = f32[512,256]{1,0:T(8,128)S(1)} all-gather(f32[32,256]{1,0:T(8,128)S(1)} %copy.22), channel_id=1, replica_groups=mesh['row'=8,'col'=16] {'col'}, dimensions={0}, use_global_device_ids=true | all-gather | bytes 557056 | tf_op jit(solution)/shard_map/all_gather | solution.py:76
  323.0 1.2 pad_maximum_fusion
  324.2 3.0 gather_fusion.1
  327.2 10.4 %fusion = f32[256,2048]{1,0:T(8,128)} fusion(f32[1,1,2048,512]{3,2,1,0:T(8,128)} %param.13, f32[512,256]{1,0:T(8,128)S(1)} %gather_fusion.1, pred[512]{0:T(512)(128)(4,1)S(1)} %compare_and_fusion), kind=kOutput, calls=%fused_computation.3 | convolution fusion | flops 3221356544 | bytes 6816256 | tf_op jit(solution)/shard_map/dot_general | solution.py:79
  337.6 6.5 %fusion.2 = f32[1,1,2048,256]{2,3,1,0:T(8,128)} fusion(f32[256,2048]{1,0:T(8,128)} %fusion, f32[256,256]{1,0:T(8,128)} %bitcast.9, f32[1,1,2048,256]{3,2,1,0:T(8,128)S(1)} %copy-done), kind=kOutput, calls=%fused_computation.6 | convolution fusion | flops 1611137024 | bytes 6553600 | tf_op jit(solution)/shard_map/dot_general | solution.py:69
  344.1 2.9 copy.24
  (69 shorter events, 4.5 us)
Async XLA Ops:
  7.2 330.4 %copy-start = (f32[1,1,2048,256]{3,2,1,0:T(8,128)S(1)}, f32[1,1,2048,256]{3,2,1,0:T(8,128)}, u32[]{:S(2)}) copy-start(f32[1,1,2048,256]{3,2,1,0:T(8,128)} %param.12) | copy-start | bytes 6291460
  7.2 5.7 %copy-start.3 = (f32[2048,16]{0,1:T(8,128)S(1)}, f32[2048,16]{0,1:T(8,128)}, u32[]{:S(2)}) copy-start(f32[2048,16]{0,1:T(8,128)} %param.8) | copy-start | bytes 393220
  7.2 139.3 %all-reduce.2.cloned.1.call-start = ((), (), s32[]{:S(2)}) async-start(), calls=%async_computation.2 | async-start | bytes 2097152 | tf_op jit(solution)/shard_map/psum | solution.py:50
  7.2 9.1 %collective-permute-start = (f32[2048,16]{0,1:T(8,128)}, f32[2048,16]{0,1:T(8,128)S(1)}, u32[]{:S(2)}, u32[]{:S(2)}) collective-permute-start(f32[2048,16]{0,1:T(8,128)} %param.8), channel_id=1, source_target_pairs={{0,1},{1,2},{2,3},{3,4},{4,5},{5,6},{6,7},{7,8},{8,9},{9,10},{10,1... | collective-permute-start | bytes 393224 | tf_op jit(solution)/shard_map/ppermute | solution.py:18
  8.9 7.4 %collective-permute-start.1 = (f32[2048,16]{0,1:T(8,128)}, f32[2048,16]{0,1:T(8,128)S(1)}, u32[]{:S(2)}, u32[]{:S(2)}) collective-permute-start(f32[2048,16]{0,1:T(8,128)} %param.8), channel_id=1, source_target_pairs={{0,15},{1,0},{2,1},{3,2},{4,3},{5,4},{6,5},{7,6},{8,7},{9,8},{10,9... | collective-permute-start | bytes 393224 | tf_op jit(solution)/shard_map/ppermute | solution.py:23
  16.3 8.3 %collective-permute-start.2 = (f32[2048,16]{0,1:T(8,128)S(1)}, f32[2048,16]{0,1:T(8,128)S(1)}, u32[]{:S(2)}, u32[]{:S(2)}) collective-permute-start(f32[2048,16]{0,1:T(8,128)S(1)} %collective-permute-done), channel_id=1, source_target_pairs={{0,1},{1,2},{2,3},{3,4},{4,5},{5,6},{6,7},{7,8},{8,9},{9,10},{10,1... | collective-permute-start | bytes 393224 | tf_op jit(solution)/shard_map/ppermute | solution.py:18
  16.3 8.3 %collective-permute-start.3 = (f32[2048,16]{0,1:T(8,128)S(1)}, f32[2048,16]{0,1:T(8,128)S(1)}, u32[]{:S(2)}, u32[]{:S(2)}) collective-permute-start(f32[2048,16]{0,1:T(8,128)S(1)} %collective-permute-done.1), channel_id=1, source_target_pairs={{0,15},{1,0},{2,1},{3,2},{4,3},{5,4},{6,5},{7,6},{8,7},{9,8},{10,9... | collective-permute-start | bytes 393224 | tf_op jit(solution)/shard_map/ppermute | solution.py:23
  24.6 8.3 %collective-permute-start.4 = (f32[2048,16]{0,1:T(8,128)S(1)}, f32[2048,16]{0,1:T(8,128)S(1)}, u32[]{:S(2)}, u32[]{:S(2)}) collective-permute-start(f32[2048,16]{0,1:T(8,128)S(1)} %collective-permute-done.2), channel_id=1, source_target_pairs={{0,1},{1,2},{2,3},{3,4},{4,5},{5,6},{6,7},{7,8},{8,9},{9,10},{10,1... | collective-permute-start | bytes 393224 | tf_op jit(solution)/shard_map/ppermute | solution.py:18
  24.6 8.3 %collective-permute-start.5 = (f32[2048,16]{0,1:T(8,128)S(1)}, f32[2048,16]{0,1:T(8,128)S(1)}, u32[]{:S(2)}, u32[]{:S(2)}) collective-permute-start(f32[2048,16]{0,1:T(8,128)S(1)} %collective-permute-done.3), channel_id=1, source_target_pairs={{0,15},{1,0},{2,1},{3,2},{4,3},{5,4},{6,5},{7,6},{8,7},{9,8},{10,9... | collective-permute-start | bytes 393224 | tf_op jit(solution)/shard_map/ppermute | solution.py:23
  32.9 8.3 %collective-permute-start.6 = (f32[2048,16]{0,1:T(8,128)S(1)}, f32[2048,16]{0,1:T(8,128)S(1)}, u32[]{:S(2)}, u32[]{:S(2)}) collective-permute-start(f32[2048,16]{0,1:T(8,128)S(1)} %collective-permute-done.4), channel_id=1, source_target_pairs={{0,1},{1,2},{2,3},{3,4},{4,5},{5,6},{6,7},{7,8},{8,9},{9,10},{10,1... | collective-permute-start | bytes 393224 | tf_op jit(solution)/shard_map/ppermute | solution.py:18
  32.9 8.3 %collective-permute-start.7 = (f32[2048,16]{0,1:T(8,128)S(1)}, f32[2048,16]{0,1:T(8,128)S(1)}, u32[]{:S(2)}, u32[]{:S(2)}) collective-permute-start(f32[2048,16]{0,1:T(8,128)S(1)} %collective-permute-done.5), channel_id=1, source_target_pairs={{0,15},{1,0},{2,1},{3,2},{4,3},{5,4},{6,5},{7,6},{8,7},{9,8},{10,9... | collective-permute-start | bytes 393224 | tf_op jit(solution)/shard_map/ppermute | solution.py:23
  41.2 8.3 %collective-permute-start.8 = (f32[2048,16]{0,1:T(8,128)S(1)}, f32[2048,16]{0,1:T(8,128)S(1)}, u32[]{:S(2)}, u32[]{:S(2)}) collective-permute-start(f32[2048,16]{0,1:T(8,128)S(1)} %collective-permute-done.6), channel_id=1, source_target_pairs={{0,1},{1,2},{2,3},{3,4},{4,5},{5,6},{6,7},{7,8},{8,9},{9,10},{10,1... | collective-permute-start | bytes 393224 | tf_op jit(solution)/shard_map/ppermute | solution.py:18
  41.2 8.3 %collective-permute-start.9 = (f32[2048,16]{0,1:T(8,128)S(1)}, f32[2048,16]{0,1:T(8,128)S(1)}, u32[]{:S(2)}, u32[]{:S(2)}) collective-permute-start(f32[2048,16]{0,1:T(8,128)S(1)} %collective-permute-done.7), channel_id=1, source_target_pairs={{0,15},{1,0},{2,1},{3,2},{4,3},{5,4},{6,5},{7,6},{8,7},{9,8},{10,9... | collective-permute-start | bytes 393224 | tf_op jit(solution)/shard_map/ppermute | solution.py:23
  49.5 8.9 %collective-permute-start.10 = (f32[2048,16]{0,1:T(8,128)S(1)}, f32[2048,16]{0,1:T(8,128)S(1)}, u32[]{:S(2)}, u32[]{:S(2)}) collective-permute-start(f32[2048,16]{0,1:T(8,128)S(1)} %collective-permute-done.8), channel_id=1, source_target_pairs={{0,1},{1,2},{2,3},{3,4},{4,5},{5,6},{6,7},{7,8},{8,9},{9,10},{10,1... | collective-permute-start | bytes 393224 | tf_op jit(solution)/shard_map/ppermute | solution.py:18
  49.5 8.9 %collective-permute-start.11 = (f32[2048,16]{0,1:T(8,128)S(1)}, f32[2048,16]{0,1:T(8,128)S(1)}, u32[]{:S(2)}, u32[]{:S(2)}) collective-permute-start(f32[2048,16]{0,1:T(8,128)S(1)} %collective-permute-done.9), channel_id=1, source_target_pairs={{0,15},{1,0},{2,1},{3,2},{4,3},{5,4},{6,5},{7,6},{8,7},{9,8},{10,9... | collective-permute-start | bytes 393224 | tf_op jit(solution)/shard_map/ppermute | solution.py:23
  58.4 9.3 %collective-permute-start.12 = (f32[2048,16]{0,1:T(8,128)S(1)}, f32[2048,16]{0,1:T(8,128)S(1)}, u32[]{:S(2)}, u32[]{:S(2)}) collective-permute-start(f32[2048,16]{0,1:T(8,128)S(1)} %collective-permute-done.10), channel_id=1, source_target_pairs={{0,1},{1,2},{2,3},{3,4},{4,5},{5,6},{6,7},{7,8},{8,9},{9,10},{10,1... | collective-permute-start | bytes 393224 | tf_op jit(solution)/shard_map/ppermute | solution.py:18
  58.4 9.3 %collective-permute-start.13 = (f32[2048,16]{0,1:T(8,128)S(1)}, f32[2048,16]{0,1:T(8,128)S(1)}, u32[]{:S(2)}, u32[]{:S(2)}) collective-permute-start(f32[2048,16]{0,1:T(8,128)S(1)} %collective-permute-done.11), channel_id=1, source_target_pairs={{0,15},{1,0},{2,1},{3,2},{4,3},{5,4},{6,5},{7,6},{8,7},{9,8},{10,9... | collective-permute-start | bytes 393224 | tf_op jit(solution)/shard_map/ppermute | solution.py:23
  67.7 8.3 %collective-permute-start.14 = (f32[2048,16]{0,1:T(8,128)S(1)}, f32[2048,16]{0,1:T(8,128)S(1)}, u32[]{:S(2)}, u32[]{:S(2)}) collective-permute-start(f32[2048,16]{0,1:T(8,128)S(1)} %collective-permute-done.12), channel_id=1, source_target_pairs={{0,1},{1,2},{2,3},{3,4},{4,5},{5,6},{6,7},{7,8},{8,9},{9,10},{10,1... | collective-permute-start | bytes 393224 | tf_op jit(solution)/shard_map/ppermute | solution.py:18
  86.4 144.5 %reduce-scatter.2.cloned.1.call-start = ((), (), s32[]{:S(2)}) async-start(), calls=%async_computation.3 | async-start | bytes 2228224 | tf_op jit(solution)/shard_map/reduce_scatter | solution.py:53
  157.3 75.3 %copy-start.6 = (s32[88,1]{0,1:T(1,128)S(1)}, s32[88,1]{0,1:T(1,128)}, u32[]{:S(2)}) copy-start(s32[88,1]{0,1:T(1,128)} %param.9) | copy-start | bytes 1060
  157.3 76.7 %copy-start.5 = (s32[1,1,512]{2,1,0:T(1,128)S(1)}, s32[1,1,512]{2,1,0:T(1,128)}, u32[]{:S(2)}) copy-start(s32[1,1,512]{2,1,0:T(1,128)} %param.11) | copy-start | bytes 6148
  157.4 140.1 %copy-start.4 = (f32[1,32,1024]{2,1,0:T(8,128)S(1)}, f32[1,32,1024]{2,1,0:T(8,128)}, u32[]{:S(2)}) copy-start(f32[1,32,1024]{2,1,0:T(8,128)} %param.10) | copy-start | bytes 393220
  157.4 140.1 %all-gather.2.cloned.1.call-start = ((), (), s32[]{:S(2)}) async-start(), calls=%async_computation.4 | async-start | bytes 1056768 | tf_op jit(solution)/shard_map/all_gather | solution.py:72
  230.9 66.7 %copy-start.2 = (f32[128,256]{0,1:T(8,128)S(1)}, f32[128,256]{0,1:T(8,128)}, u32[]{:S(2)}) copy-start(f32[128,256]{0,1:T(8,128)} %reduce-scatter.2.cloned.1.call-done) | copy-start | bytes 393220
  236.9 100.7 %all-to-all-start = ((f32[16,16,256]{2,1,0:T(8,128)}), f32[16,16,256]{2,1,0:T(8,128)}, u32[]{:S(2)}, u32[]{:S(2)}) async-start(f32[16,16,256]{2,1,0:T(8,128)} %broadcast_select_fusion), calls=%async_computation.1 | async-start | bytes 524288 | tf_op jit(solution)/shard_map/all_to_all | solution.py:67
  297.5 25.5 %copy-start.1 = (f32[1024,256]{1,0:T(8,128)S(1)}, f32[1024,256]{1,0:T(8,128)}, u32[]{:S(2)}) copy-start(f32[1024,256]{1,0:T(8,128)} %all-gather.2.cloned.1.call-done) | copy-start | bytes 3145732
Sparse Core Ops, SparseCore 0:
  86.5 59.8 all-reduce.1
  157.5 73.3 reduce-scatter.1
  234.6 62.8 all-gather.1
